TPU v7x, 256 devices: a whole 4x4x8 slice. The times are simulated.
256 devices in a mesh: fsdp: 32 (over x, y, core), dp: 8 (over z).
Axes of the slice: x: 4, y: 4, z: 8, core: 2. Of those that a mesh axis runs over, the one named last changes fastest.
Arguments:
- tokens: bfloat16 [32, 2048, 8192], P('fsdp', 'dp'), may hold values from -6 to 6
- norm_gain: float32 [8192], replicated, may hold values from 0.6 to 35
- old_master: float32 [3072, 2048], P('fsdp'), may hold values from -0.0625 to 0.0625
- route_peer: int32 [32, 96], replicated, may hold values from 0 to 31, as said below
- route_slot: int32 [32, 96], replicated, may hold values from 0 to 95
- out_weight: bfloat16 [512, 8192], P(None, 'fsdp'), may hold values from -1.5 to 1.5
- doc_lengths: int32 [32, 8], P('fsdp'), may hold values from 1 to 1024, 2048 in all within a row
Outputs:
- attn_update: bfloat16 [32, 2048, 8192], P('fsdp', 'dp')
- new_master: float32 [3072, 2048], P('fsdp')
Inputs may be any that keep to these rules, and one draw needn't show every extreme that they name: For every old owner i and every new owner j, route_peer[i, p] == j for at most 6 positions p, and for exactly 6 of them with one j per i; every new owner receives exactly 96 blocks, one for each slot, so (route_peer, route_slot) is a bijection onto owner and slot.
All inputs are finite; a program needn't handle non-finite values.
Results may differ from a plain program's by a relative error of at most 0.0095.
The roundings to bfloat16 on the way count: a program that leaves them out, or rounds other values in their place, can miss the bound.
Values may be sent and summed in bfloat16 or wider, within the bound.
A program may use at most 128 MiB of HBM per device.

v0:
```python
import jax
import jax.numpy as jnp
from jax import lax
from jax.sharding import PartitionSpec as P

HD = 128
HQ = 4
BLK = 2048


theta_base = 500000.0
epsilon = 1e-05
masked_score = -1e30


def rope_tables(positions):
    half_size = HD // 2
    inverse = jnp.exp(
        -jnp.log(jnp.float32(theta_base)) * jnp.arange(half_size, dtype=jnp.float32) * 2.0 / HD
    )
    angles = positions.astype(jnp.float32)[:, None] * inverse[None, :]
    return (jnp.cos(angles), jnp.sin(angles))


def rotate(values, cosine, sine):
    half_size = HD // 2
    first = values[..., :half_size]
    second = values[..., half_size:]
    return jnp.concatenate(
        [first * cosine - second * sine, second * cosine + first * sine], axis=-1
    )


def per_device(tokens, norm_gain, old_master, route_peer, route_slot, out_weight, doc_lengths):
    groups = lax.axis_size("fsdp")
    member = lax.axis_index("fsdp")
    blocks = old_master.shape[0]
    most_rows = max(2, 2 * blocks // groups)
    width = (HQ + 2) * HD
    out_rows = HQ * HD
    own_peer = lax.dynamic_index_in_dim(route_peer, member, 0, keepdims=False)
    block_index = jnp.arange(blocks)
    earlier = (own_peer[:, None] == own_peer[None, :]) & (
        block_index[None, :] < block_index[:, None]
    )
    sending_rank = jnp.sum(earlier.astype(jnp.int32), axis=1)
    outgoing = (
        jnp.zeros((groups, most_rows, BLK), jnp.float32).at[own_peer, sending_rank].set(old_master)
    )
    incoming = lax.all_to_all(
        outgoing.astype(jnp.bfloat16), "fsdp", split_axis=0, concat_axis=0, tiled=True
    ).astype(outgoing.dtype)
    inbound = route_peer == member
    arrival = jnp.cumsum(inbound.astype(jnp.int32), axis=1) - 1
    source_row = jnp.where(
        inbound, jnp.arange(groups, dtype=jnp.int32)[:, None] * most_rows + arrival, 0
    )
    target_slot = jnp.where(inbound, route_slot, blocks)
    slot_source = (
        jnp.zeros((blocks,), jnp.int32)
        .at[target_slot.reshape(-1)]
        .set(source_row.reshape(-1), mode="drop")
    )
    new_master = incoming.reshape(groups * most_rows, BLK)[slot_source]
    sequence = tokens[0]
    rows_local = sequence.shape[0]
    values_f = sequence.astype(jnp.float32)
    square_mean = jnp.mean(values_f * values_f, axis=-1, keepdims=True)
    normed = (values_f * lax.rsqrt(square_mean + epsilon) * norm_gain).astype(jnp.bfloat16)
    panel = new_master.astype(jnp.bfloat16).reshape(-1, width)
    projection = jnp.dot(
        normed,
        lax.all_gather(panel, "fsdp", axis=0, tiled=True),
        preferred_element_type=jnp.float32,
    )
    seat = lax.axis_index("dp")
    first_query = seat * rows_local
    query_pos = first_query + jnp.arange(rows_local, dtype=jnp.int32)
    cosine, sine = rope_tables(query_pos)
    queries = projection[:, :out_rows].reshape(rows_local, HQ, HD)
    queries = rotate(queries, cosine[:, None, :], sine[:, None, :]).astype(jnp.bfloat16)
    queries = jnp.transpose(queries, (1, 0, 2)).reshape(HQ * rows_local, HD)
    keys = rotate(projection[:, out_rows : out_rows + HD], cosine, sine).astype(jnp.bfloat16)
    values = projection[:, out_rows + HD :].astype(jnp.bfloat16)
    doc_ends = jnp.cumsum(doc_lengths[0])

    def doc_of(where_at):
        return jnp.sum((where_at[..., None] >= doc_ends).astype(jnp.int32), axis=-1)

    query_rows = jnp.tile(query_pos, HQ)
    query_doc = doc_of(query_rows)
    scale = 1.0 / jnp.sqrt(jnp.float32(HD))
    best = jnp.full((HQ * rows_local, 1), masked_score, jnp.float32)
    key_part = lax.all_gather(keys, "dp", axis=0, tiled=True)
    value_part = lax.all_gather(values, "dp", axis=0, tiled=True)
    key_pos = jnp.arange(key_part.shape[0], dtype=jnp.int32)
    visible = (key_pos[None, :] <= query_rows[:, None]) & (
        doc_of(key_pos)[None, :] == query_doc[:, None]
    )
    scores = (
        lax.dot_general(
            queries, key_part, (((1,), (1,)), ((), ())), preferred_element_type=jnp.float32
        )
        * scale
    )
    scores = jnp.where(visible, scores, masked_score)
    new_best = jnp.maximum(best, jnp.max(scores, axis=1, keepdims=True))
    expterm = jnp.where(visible, jnp.exp(scores - new_best), 0.0)
    denom = jnp.sum(expterm, axis=1, keepdims=True)
    accum = jnp.dot(expterm.astype(jnp.bfloat16), value_part, preferred_element_type=jnp.float32)
    best, denom, accum = (new_best, denom, accum)
    attended = (accum / denom).reshape(HQ, rows_local, HD)
    attended = jnp.transpose(attended, (1, 0, 2)).reshape(rows_local, out_rows).astype(jnp.bfloat16)
    update = jnp.dot(
        attended,
        lax.all_gather(out_weight, "fsdp", axis=1, tiled=True),
        preferred_element_type=jnp.float32,
    )
    return (update.astype(jnp.bfloat16)[None], new_master)


def solution(mesh):
    placed = (
        P("fsdp", "dp", None),
        P(),
        P("fsdp", None),
        P(),
        P(),
        P(None, "fsdp"),
        P("fsdp", None),
    )
    return jax.shard_map(
        per_device,
        mesh=mesh,
        in_specs=placed,
        out_specs=(P("fsdp", "dp", None), P("fsdp", None)),
        check_vma=False,
    )
```

profile of v0, /device:TPU:2, one launch (start us, length us, event | category | flops | bytes accessed | tf_op | source)
XLA Modules:
  0.0 203.9 jit_solution(1191593384977740027)
XLA Ops:
  7.2 0.7 fusion.26
  7.9 0.2 convert_reduce_fusion.1
  8.0 0.7 fusion.23
  8.8 0.2 broadcast_in_dim.21
  8.9 0.0 copy-start.1
  8.9 0.0 copy-start.2
  8.9 11.5 %scatter_fusion = f32[32,6,2048]{2,0,1:T(8,128)S(1)} fusion(f32[32,6,2048]{2,0,1:T(8,128)S(1)} %broadcast_in_dim.21, s32[96]{0:T(128)S(1)} %fusion.23, f32[96,2048]{1,0:T(8,128)} %param.9), kind=kCustom, calls=%fused_computation.1 | custom fusion | bytes 2360064 | tf_op jit(solution)/shard_map/scatter | solution.py:48
  20.5 0.1 convert_element_type.66
  20.6 0.0 copy-start.4
  20.6 1.4 copy.17
  22.0 7.6 %all-to-all-start = ((bf16[32,6,2048]{2,1,0:T(8,128)(2,1)}), bf16[32,6,2048]{2,1,0:T(8,128)(2,1)S(1)}, u32[]{:S(2)}, u32[]{:S(2)}) async-start(bf16[32,6,2048]{2,1,0:T(8,128)(2,1)} %copy.17), calls=%async_computation | async-start | bytes 2097152 | tf_op jit(solution)/shard_map/all_to_all | solution.py:50
  29.6 0.0 all-gather.3.cloned.1.call-start
  29.7 0.0 copy-done.1
  29.7 0.0 copy-start.3
  29.7 0.3 reduce_window_sum.18
  30.0 0.0 copy-done.2
  30.0 0.1 add_select_fusion
  30.1 0.1 reshape.213
  30.1 0.1 reshape.238
  30.2 11.8 %scatter_custom_fusion.1 = s32[96]{0:T(128)S(1)} fusion(s32[3072]{0:T(1024)S(1)} %bitcast.47, s32[3072]{0:T(1024)S(1)} %reshape.238, s32[]{:T(128)} %constant.19.clone.1), kind=kCustom, calls=%fused_computation.58 | custom fusion | bytes 388 | tf_op jit(solution)/shard_map/scatter | solution.py:62
  42.0 2.0 all-to-all-done
  44.1 0.2 reshape.219
  44.3 0.9 gather_fusion
  45.1 0.0 copy-start
  45.2 1.2 convert_element_type.69
  46.4 0.0 all-gather.3.cloned.1.call-update
  46.4 0.0 all-gather.5.cloned.1.call-start
  46.5 0.7 all-gather.5.cloned.1.call-update
  47.2 0.0 copy-done.4
  47.2 0.2 reduce-window.8
  47.4 0.1 convert_reduce_fusion
  47.5 0.1 convert_reduce_fusion.2
  47.6 3.1 %fusion.1 = f32[256]{0:T(256)S(1)} fusion(bf16[1,256,8192]{2,1,0:T(8,128)(2,1)} %param.7), kind=kLoop, calls=%fused_computation.7 | loop fusion | flops 6291200 | bytes 4195328 | tf_op jit(solution)/shard_map/reduce_sum | solution.py:68
  50.7 65.5 %all-gather.3.cloned.1.call-done = bf16[8192,768]{1,0:T(8,128)(2,1)} async-done(((bf16[256,768]{1,0:T(8,128)(2,1)}), bf16[8192,768]{1,0:T(8,128)(2,1)}) %all-gather.3.cloned.1.call-update) | async-done | bytes 12582928 | tf_op jit(solution)/shard_map/all_gather | solution.py:73
  116.3 0.0 copy-done.3
  116.3 9.0 %fusion.8 = f32[256,768]{1,0:T(8,128)S(1)} fusion(bf16[8192,768]{1,0:T(8,128)(2,1)} %all-gather.3.cloned.1.call-done, bf16[1,256,8192]{2,1,0:T(8,128)(2,1)} %param.7, f32[8192]{0:T(1024)S(1)} %copy-done.3, f32[256]{0:T(256)S(1)} %add_rsqrt_fusion), kind=kOutput, calls=%fused_computation.17 | convolution fusion | flops 3229614080 | bytes 17597440 | tf_op jit(solution)/shard_map/dot_general | solution.py:71
  125.3 0.0 copy-done
  125.3 0.1 slice.32
  125.4 0.2 reshape.215
  125.6 0.6 subtract_convert_fusion.1
  126.2 0.1 pad_maximum_fusion.1
  126.3 0.3 fusion.32
  126.6 0.1 subtract_convert_fusion
  126.7 0.1 pad_maximum_fusion
  126.9 26.7 %all_gather.13 = bf16[2048,128]{1,0:T(8,128)(2,1)S(1)} all-gather(bf16[256,128]{1,0:T(8,128)(2,1)S(1)} %pad_maximum_fusion.1), channel_id=1, replica_groups=mesh['fsdp'=32,'dp'=8] {'dp'}, dimensions={0}, use_global_device_ids=true | all-gather | bytes 589824 | tf_op jit(solution)/shard_map/all_gather | solution.py:94
  153.6 2.5 %fusion.5 = (f32[1024]{0:T(1024)S(1)}, f32[1024,2048]{1,0:T(8,128)S(1)}) fusion(s32[2048]{0:T(1024)S(1)} %convert_reduce_fusion, s32[1024]{0:T(1024)S(1)} %bitcast.44, s32[1024]{0:T(1024)S(1)} %convert_reduce_fusion.2, bf16[1024,128]{1,0:T(8,128)(2,1)S(1)} %bitcast.41, bf16[2048,128]{1,0:T(8,128)(2,1)S(1)} %all_gather.13), kind=kOutput, calls=%fused_computation.14 | convolution fusion | flops 549452800 | bytes 9195520 | tf_op jit(solution)/shard_map/dot_general | solution.py:101
  156.1 25.7 %all_gather.14 = bf16[2048,128]{1,0:T(8,128)(2,1)S(1)} all-gather(bf16[256,128]{1,0:T(8,128)(2,1)S(1)} %slice.43), channel_id=1, replica_groups=mesh['fsdp'=32,'dp'=8] {'dp'}, dimensions={0}, use_global_device_ids=true | all-gather | bytes 589824 | tf_op jit(solution)/shard_map/all_gather | solution.py:95
  181.9 3.4 %fusion.6 = f32[1024]{0:T(1024)S(1)} fusion(f32[1024,2048]{1,0:T(8,128)S(1)} %get-tuple-element.15, f32[1024]{0:T(1024)S(1)} %broadcast_maximum_fusion, s32[2048]{0:T(1024)S(1)} %convert_reduce_fusion, s32[1024]{0:T(1024)S(1)} %bitcast.45, s32[1024]{0:T(1024)S(1)} %convert_reduce_fusion.2), kind=kLoop, calls=%fused_computation.15 | loop fusion | flops 16776192 | bytes 8413184 | tf_op jit(solution)/shard_map/reduce_sum | solution.py:109
  185.3 3.8 %fusion.18 = bf16[1024,128]{1,0:T(8,128)(2,1)S(1)} fusion(bf16[2048,128]{1,0:T(8,128)(2,1)S(1)} %all_gather.14, f32[1024,2048]{1,0:T(8,128)S(1)} %get-tuple-element.15, f32[1024]{0:T(1024)S(1)} %broadcast_maximum_fusion, s32[2048]{0:T(1024)S(1)} %convert_reduce_fusion, s32[1024]{0:T(1024)S(1)} %bitcast.46, s32[1024]{0:T(1024)S(1)} %convert_reduce_fusion.2, ...), kind=kOutput, calls=%fused_computation.23 | convolution fusion | flops 553910272 | bytes 9199616 | tf_op jit(solution)/shard_map/dot_general | solution.py:110
  189.1 0.1 copy.20
  189.2 0.0 all-gather.5.cloned.1.call-done
  189.2 7.8 %fusion = bf16[1,256,8192]{2,1,0:T(8,128)(2,1)} fusion(bf16[256,512]{0,1:T(8,128)(2,1)S(1)} %bitcast.40, bf16[512,8192]{1,0:T(8,128)(2,1)} %all-gather.5.cloned.1.call-done), kind=kOutput, calls=%fused_computation.6 | convolution fusion | flops 2149580800 | bytes 12845056 | tf_op jit(solution)/shard_map/dot_general | solution.py:114
  (14 shorter events, 0.1 us)
Async XLA Ops:
  8.9 20.8 %copy-start.1 = (s32[32,96]{1,0:T(8,128)S(1)}, s32[32,96]{1,0:T(8,128)}, u32[]{:S(2)}) copy-start(s32[32,96]{1,0:T(8,128)} %param.10) | copy-start | bytes 36868
  8.9 21.1 %copy-start.2 = (s32[32,96]{1,0:T(8,128)S(1)}, s32[32,96]{1,0:T(8,128)}, u32[]{:S(2)}) copy-start(s32[32,96]{1,0:T(8,128)} %param.11) | copy-start | bytes 36868
  20.6 26.6 %copy-start.4 = (s32[1,8]{1,0:T(1,128)S(1)}, s32[1,8]{1,0:T(1,128)}, u32[]{:S(2)}) copy-start(s32[1,8]{1,0:T(1,128)} %param.13) | copy-start | bytes 100
  22.0 22.1 %all-to-all-start = ((bf16[32,6,2048]{2,1,0:T(8,128)(2,1)}), bf16[32,6,2048]{2,1,0:T(8,128)(2,1)S(1)}, u32[]{:S(2)}, u32[]{:S(2)}) async-start(bf16[32,6,2048]{2,1,0:T(8,128)(2,1)} %copy.17), calls=%async_computation | async-start | bytes 2097152 | tf_op jit(solution)/shard_map/all_to_all | solution.py:50
  29.6 86.6 %all-gather.3.cloned.1.call-start = ((), (), s32[]{:S(2)}) async-start(), calls=%async_computation.1 | async-start | bytes 12976128 | tf_op jit(solution)/shard_map/all_gather | solution.py:73
  29.7 86.6 %copy-start.3 = (f32[8192]{0:T(1024)S(1)}, f32[8192]{0:T(1024)}, u32[]{:S(2)}) copy-start(f32[8192]{0:T(1024)} %param.8) | copy-start | bytes 98308
  45.1 80.1 %copy-start = (f32[96,2048]{1,0:T(8,128)}, f32[96,2048]{1,0:T(8,128)S(1)}, u32[]{:S(2)}) copy-start(f32[96,2048]{1,0:T(8,128)S(1)} %gather_fusion) | copy-start | bytes 2359300
  46.4 142.8 %all-gather.5.cloned.1.call-start = ((), (), s32[]{:S(2)}) async-start(), calls=%async_computation.2 | async-start | bytes 8650752 | tf_op jit(solution)/shard_map/all_gather | solution.py:116
Sparse Core Ops, SparseCore 0:
  46.5 69.6 all-gather.2
  118.7 63.8 all-gather.4
where the time goes:
time: 204 us
  waiting for transfers between devices  68.3 us (33%)
  blocking collectives  52.5 us (26%)
  local copies, waits for them, and re-layouts  28.7 us (14%)
  matrix products  23.1 us (11%)
  between operations  14.3 us (7%)
  other arithmetic  9.26 us (5%)
  starting transfers between devices  7.69 us (4%)
    all_gather x1, waiting for transfers between devices, per_device(): lax.all_gather(panel, 'fsdp', axis=0, tiled=True)  65.5 us
    all_gather x1, blocking collectives, per_device(): key_part = lax.all_gather(keys, 'dp', axis=0, tiled=True)  26.7 us
    all_gather x1, blocking collectives, per_device(): value_part = lax.all_gather(values, 'dp', axis=0, tiled=True)  25.7 us
    scatter x1, local copies, waits for them, and re-layouts, per_device(): slot_source = jnp.zeros((blocks,), jnp.int32).at[target_slot.reshape(-1)]...  11.8 us
    scatter x1, local copies, waits for them, and re-layouts, per_device(): jnp.zeros((groups, most_rows, BLK), jnp.float32).at[own_peer, sending_rank]  11.5 us
    dot_general x1, matrix products, per_device(): jnp.dot(normed, lax.all_gather(panel, 'fsdp', axis=0, tiled=True), prefer...  9.03 us
    dot_general x1, matrix products, per_device(): jnp.dot(attended, lax.all_gather(out_weight, 'fsdp', axis=1, tiled=True),...  7.77 us
    all_to_all x1, starting transfers between devices, per_device(): lax.all_to_all(outgoing.astype(jnp.bfloat16), 'fsdp', split_axis=0, conca...  7.61 us
  transfers between devices with their start and end apart: 3, of which 2 were waited for; matrix products, arithmetic and copies ran while one was open for 18% of the time, Pallas kernels for 0%

commit v1 on v0

v1 whole, which is shorter than its diff:
```python
import jax
import jax.numpy as jnp
import numpy as np
from jax import lax
from jax.experimental import pallas as pl
from jax.experimental.pallas import tpu as pltpu
from jax.sharding import PartitionSpec as P

HD = 128
HQ = 4
BLK = 2048
theta_base = 500000.0
epsilon = 1e-05
masked_score = -1e30
MESH = pl.DeviceIdType.MESH
F32, BF16, I32 = jnp.float32, jnp.bfloat16, jnp.int32

NF, NZ = 32, 8
ROWS, D = 256, 8192
QW, KVW, W = 512, 256, 768
LANES = 128
COLS = ((QW, KVW), (0, QW))
BACK = 4


def dot(a, b):
    return jnp.dot(a, b, preferred_element_type=F32)


def iota(shape, axis):
    return lax.broadcasted_iota(I32, shape, axis)


def hot(condition):
    return jnp.where(condition, 1.0, 0.0).astype(BF16)


def kernel(
    tok_hbm, gain, old, peer, slot, ow_hbm, docs, cos_r, sin_r, cos_z, sin_z,
    out_hbm, nm_hbm,
    tok, oldb, sendbuf, inbuf, wbuf, obuf, kvbuf, acc, att, staged, nm, bias,
    local_sem, a2a_s, a2a_r, w_s, w_r, sib_s, sib_r, ow_s, ow_r, oz_s, oz_r, os_s, os_r, kv_s, kv_r, out_sem,
):
    me = lax.axis_index("fsdp")
    z = lax.axis_index("dp")
    c = lax.rem(me, 2)
    y = lax.rem(lax.div(me, 2), 4)
    x = lax.div(me, 8)
    place = x * 4 + y
    sibling = me + 1 - 2 * c
    up, down = lax.rem(z + 1, NZ), lax.rem(z + NZ - 1, NZ)

    def panel(dx, dy, core):
        return lax.rem(x + 4 - dx, 4) * 8 + lax.rem(y + 4 - dy, 4) * 2 + core

    def remote(src, dst, send, recv, **to):
        return pltpu.make_async_remote_copy(
            src_ref=src, dst_ref=dst, send_sem=send, recv_sem=recv, device_id=to, device_id_type=MESH
        )

    barrier = pltpu.get_barrier_semaphore()

    @pl.loop(1, NF)
    def _(k):
        pl.semaphore_signal(barrier, inc=1, device_id={"fsdp": lax.rem(me + k, NF)}, device_id_type=MESH)

    for to in (up, down):
        pl.semaphore_signal(barrier, inc=1, device_id={"dp": to}, device_id_type=MESH)

    tokens_in = pltpu.make_async_copy(tok_hbm, tok, local_sem.at[0])
    tokens_in.start()
    own_rows = pl.ds(pl.multiple_of(z * 64, 64), 64)
    own_out = pltpu.make_async_copy(ow_hbm.at[own_rows, :], obuf.at[c, place, own_rows, :], local_sem.at[1])
    own_out.start()

    for part in range(8):
        oldb[pl.ds(part * LANES, 96), :] = old[:, pl.ds(part * 256, 256)].astype(BF16)
        oldb[pl.ds(part * LANES + 96, 32), :] = jnp.zeros((32, 256), BF16)
    before = hot(iota((LANES, LANES), 0) < iota((LANES, LANES), 1))
    own_peer = peer[pl.ds(me, 1), :]
    mine = iota((NF, LANES), 0) == own_peer
    rank = jnp.sum(jnp.where(mine, dot(hot(mine), before), 0.0), axis=0, keepdims=True).astype(I32)
    base = jnp.where(own_peer >= 0, own_peer * 16 + (rank & 1) * 8, -1000)
    for g in range(3):
        target = jnp.where((rank >> 1) == g, base, -1000)
        rows = iota((NF * 16, LANES), 0)
        select = jnp.concatenate([hot(rows == target + part) for part in range(8)], axis=1)
        sendbuf[:, pl.ds(g * 256, 256)] = dot(select, oldb[...]).astype(BF16)

    pl.semaphore_wait(barrier, NF - 1 + 2)

    def sixteen(f):
        return pl.ds(pl.multiple_of(f * 16, 16), 16)

    def a2a(to):
        return remote(
            sendbuf.at[sixteen(to), :], inbuf.at[sixteen(me), :], a2a_s.at[to], a2a_r.at[me], fsdp=to
        )

    def a2a_from(f):
        return remote(
            sendbuf.at[sixteen(f), :], inbuf.at[sixteen(f), :], a2a_s.at[f], a2a_r.at[f], fsdp=f
        )

    @pl.loop(1, NF)
    def _(k):
        a2a(lax.rem(me + k, NF)).start()

    inbuf[sixteen(me), :] = sendbuf[sixteen(me), :]

    def ow_to(k):
        to = lax.rem(place + k, 16)
        return remote(
            ow_hbm.at[own_rows, :], obuf.at[c, place, own_rows, :], ow_s.at[to], ow_r.at[place], fsdp=to * 2 + c
        )

    def ow_from(f):
        return remote(
            ow_hbm.at[own_rows, :], obuf.at[c, f, own_rows, :], ow_s.at[f], ow_r.at[f], fsdp=f * 2 + c
        )

    @pl.loop(1, 16)
    def _(k):
        ow_to(k).start()

    tokens_in.wait()

    @pl.loop(0, ROWS // 16)
    def _(i):
        rows = pl.ds(pl.multiple_of(i * 16, 16), 16)
        values = tok[rows, :].astype(F32)
        square_mean = jnp.mean(values * values, axis=-1, keepdims=True)
        tok[rows, :] = (values * lax.rsqrt(square_mean + epsilon) * gain[...]).astype(BF16)

    ours = peer[...] == me
    arrival = dot(hot(ours), before)
    lane = iota((1, NF * 16), 1)
    holder = iota((NF, NF * 16), 0) == (iota((NF, NF * 16), 1) >> 4)
    odd = ((iota((NF, NF * 16), 1) >> 3) & 1) == 1
    slots = []
    for r in range(6):
        found = ours & (arrival == float(r))
        slots.append(jnp.sum(jnp.where(found, slot[...] + 1, 0), axis=1, keepdims=True) - 1)
    slot_rows = []
    for g in range(3):
        spread = jnp.where(odd, slots[2 * g + 1], slots[2 * g])
        slot_rows.append(jnp.sum(jnp.where(holder, spread, 0), axis=0, keepdims=True))

    @pl.loop(1, NF)
    def _(k):
        a2a_from(lax.rem(me + NF - k, NF)).wait_recv()

    def panel_rows(f):
        return pl.ds(pl.multiple_of(f * ROWS, ROWS), ROWS)

    for g in range(3):
        total = jnp.zeros((256, 256), F32)
        for h in range(3):
            flat = slot_rows[h] * 8 + (lane & 7)
            row = (flat * 21846) >> 16
            row = jnp.where((slot_rows[h] >= 0) & (flat - row * 3 == g), row, -1)
            total += dot(hot(iota((256, NF * 16), 0) == row), inbuf[:, pl.ds(h * 256, 256)])
        wbuf[panel_rows(me), pl.ds(g * 256, 256)] = total.astype(BF16)

    def coords(half, first, second):
        return (first, second) if half == 0 else (second, first)

    def neighbour(axis, step):
        if axis == 0:
            return lax.rem(x + 4 + step, 4) * 8 + y * 2 + c
        return x * 8 + lax.rem(y + 4 + step, 4) * 2 + c

    def ring(stage, half, phase, kind, sending):
        step = 1 if kind in (0, 2) else -1
        arrives = {0: 1, 1: 3, 2: 2, 3: 2}[kind]
        leaves = {0: 0, 1: 0, 2: 1, 3: 3}[kind]
        along = leaves if sending else arrives
        if phase == 0:
            dx, dy = coords(half, along, 0)
            axis = half
        else:
            dx, dy = coords(half, phase - 1, along)
            axis = 1 - half
        start = panel(dx, dy, c) * ROWS + half * 128 + (64 if kind == 3 else 0)
        size = 64 if kind >= 2 else 128
        first, width = COLS[stage]
        ref = wbuf.at[pl.ds(pl.multiple_of(start, 64), size), pl.ds(first, width)]
        index = ((stage * 2 + half) * 5 + phase) * 4 + kind
        return remote(ref, ref, w_s.at[index], w_r.at[index], fsdp=neighbour(axis, step))

    def go(stage, phase, kinds):
        for kind in kinds:
            for half in range(2):
                ring(stage, half, phase, kind, True).start()

    def come(stage, phase, kinds):
        for kind in kinds:
            for half in range(2):
                ring(stage, half, phase, kind, False).wait_recv()

    def side(stage, dx, dy, core):
        first, width = COLS[stage]
        ref = wbuf.at[panel_rows(panel(dx, dy, core)), pl.ds(first, width)]
        index = stage * 16 + dx * 4 + dy
        return remote(ref, ref, sib_s.at[index], sib_r.at[index], fsdp=sibling)

    def share(stage, places):
        for dx, dy in places:
            side(stage, dx, dy, c).start()

    def multiply(stage, places, other):
        first, width = COLS[stage]
        for dx, dy in places:
            if other:
                side(stage, dx, dy, 1 - c).wait_recv()
            f = panel(dx, dy, 1 - c if other else c)
            columns = pl.ds(first, width)
            acc[:, columns] += dot(tok[:, panel_rows(f)], wbuf[panel_rows(f), columns])

    near = [(0, 0)]
    cross = [(1, 0), (3, 0), (0, 1), (0, 3)]
    corner = [(1, 1), (1, 3), (3, 1), (3, 3)]
    two = [(2, 0), (0, 2)]
    knight = [(1, 2), (3, 2), (2, 1), (2, 3)]
    far = [(2, 2)]

    def open_stage(stage):
        go(stage, 0, (0, 1))
        go(stage, 1, (0, 1))
        share(stage, near)

    def step_one(stage):
        come(stage, 0, (0,))
        go(stage, 0, (2,))
        go(stage, 2, (0, 1))
        come(stage, 0, (1,))
        go(stage, 0, (3,))
        go(stage, 4, (0, 1))

    def step_two(stage):
        come(stage, 1, (0,))
        go(stage, 1, (2,))
        come(stage, 1, (1,))
        go(stage, 1, (3,))
        share(stage, cross)

    def step_three(stage):
        come(stage, 0, (2, 3))
        go(stage, 3, (0, 1))

    def step_four(stage):
        for phase in (2, 4):
            come(stage, phase, (0,))
            go(stage, phase, (2,))
            come(stage, phase, (1,))
            go(stage, phase, (3,))
        share(stage, corner)

    def step_five(stage):
        come(stage, 1, (2, 3))
        share(stage, two)
        come(stage, 3, (0,))
        go(stage, 3, (2,))
        come(stage, 3, (1,))
        go(stage, 3, (3,))

    def step_six(stage):
        come(stage, 2, (2, 3))
        come(stage, 4, (2, 3))
        share(stage, knight)

    def step_seven(stage):
        come(stage, 3, (2, 3))
        share(stage, far)

    def oz(way, step, sending):
        at = z - (step - 1 if sending else step) if way == 0 else z + (step - 1 if sending else step)
        rows = pl.ds(pl.multiple_of(lax.rem(at + NZ, NZ) * 64, 64), 64)
        ref = obuf.at[c, :, rows, :]
        index = way * 4 + step - 1
        return remote(ref, ref, oz_s.at[index], oz_r.at[index], dp=up if way == 0 else down)

    def o_side(back, core):
        rows = pl.ds(pl.multiple_of(lax.rem(z + NZ - back, NZ) * 64, 64), 64)
        ref = obuf.at[core, :, rows, :]
        return remote(ref, ref, os_s.at[back], os_r.at[back], fsdp=sibling)

    def oz_next(step):
        if step <= 3:
            oz(0, step, False).wait_recv()
            if step < 3:
                oz(0, step + 1, True).start()
            o_side(step, c).start()
        oz(1, step, False).wait_recv()
        if step < 4:
            oz(1, step + 1, True).start()
        o_side(NZ - step, c).start()

    def kv(step, sending):
        src = kvbuf.at[pl.ds((step - 1) * ROWS, ROWS), :]
        dst = kvbuf.at[pl.ds(step * ROWS, ROWS), :]
        return remote(src, dst, kv_s.at[step - 1], kv_r.at[step - 1], dp=up)

    open_stage(0)

    @pl.loop(1, 16)
    def _(k):
        ow_from(lax.rem(place + 16 - k, 16)).wait_recv()

    own_out.wait()
    oz(0, 1, True).start()
    oz(1, 1, True).start()
    o_side(0, c).start()

    step_one(0)
    acc[...] = jnp.zeros_like(acc)
    for part in range(8):
        total = jnp.zeros((96, 256), F32)
        for h in range(3):
            row = jnp.where((lane & 7) == part, slot_rows[h], -1)
            total += dot(hot(iota((96, NF * 16), 0) == row), inbuf[:, pl.ds(h * 256, 256)])
        nm[:, pl.ds(part * 256, 256)] = total
    nm_out = pltpu.make_async_copy(nm, nm_hbm, local_sem.at[2])
    nm_out.start()
    step_two(0)
    multiply(0, near, False)
    step_three(0)
    multiply(0, near, True)
    open_stage(1)
    step_four(0)
    multiply(0, cross, False)
    step_five(0)
    multiply(0, cross, True)
    multiply(0, corner, False)
    step_one(1)
    step_six(0)
    oz_next(1)
    multiply(0, corner + two, True)
    multiply(0, two, False)
    step_two(1)
    step_seven(0)
    multiply(0, knight + far, False)
    step_three(1)
    multiply(0, knight + far, True)

    cz, sz = cos_z[pl.ds(z, 1), :], sin_z[pl.ds(z, 1), :]
    cosine = cos_r[...] * cz - sin_r[...] * sz
    sine = sin_r[...] * cz + cos_r[...] * sz
    sine = jnp.where(iota((ROWS, HD), 1) < HD // 2, -sine, sine)

    def rotate(values):
        return (values * cosine + pltpu.roll(values, HD // 2, 1) * sine).astype(BF16)

    kvbuf[pl.ds(0, ROWS), pl.ds(0, HD)] = rotate(acc[:, pl.ds(QW, HD)])
    kvbuf[pl.ds(0, ROWS), pl.ds(HD, HD)] = acc[:, pl.ds(QW + HD, HD)].astype(BF16)
    kv(1, True).start()
    step_four(1)
    multiply(1, near + cross, False)
    kv(1, False).wait_recv()
    kv(2, True).start()
    step_five(1)
    oz_next(2)
    multiply(1, near + cross, True)
    kv(2, False).wait_recv()
    kv(3, True).start()
    multiply(1, corner + two, False)
    step_six(1)
    multiply(1, corner + two, True)
    kv(3, False).wait_recv()
    kv(4, True).start()

    query = z * ROWS + iota((ROWS, 1), 0)
    begin = jnp.zeros((ROWS, 1), I32)
    end = jnp.int32(0)
    for d in range(8):
        end = end + docs[0, d]
        begin = jnp.where(query >= end, end, begin)
    for back in range(BACK + 1):
        key = (z - back) * ROWS + iota((ROWS, ROWS), 1)
        bias[:, pl.ds(back * ROWS, ROWS)] = jnp.where((key <= query) & (key >= begin), 0.0, masked_score)

    step_seven(1)
    oz_next(3)
    multiply(1, knight + far, False)
    multiply(1, knight + far, True)
    kv(4, False).wait_recv()

    scale = 1.0 / np.sqrt(np.float32(HD))
    for h in range(HQ):
        columns = pl.ds(h * HD, HD)
        queries = rotate(acc[:, columns])
        scores = lax.dot_general(
            queries, kvbuf[:, pl.ds(0, HD)], (((1,), (1,)), ((), ())), preferred_element_type=F32
        )
        scores = scores * scale + bias[...]
        expterm = jnp.exp(scores - jnp.max(scores, axis=1, keepdims=True))
        denom = jnp.sum(expterm, axis=1, keepdims=True)
        att[:, columns] = (dot(expterm.astype(BF16), kvbuf[:, pl.ds(HD, HD)]) / denom).astype(BF16)

    oz_next(4)
    for back in range(NZ):
        o_side(back, 1 - c).wait_recv()

    def out_copy(part):
        columns = pl.ds(part * 2048, 2048)
        return pltpu.make_async_copy(staged.at[:, columns], out_hbm.at[:, columns], out_sem.at[part])

    for part in range(4):
        for i in range(8):
            f = part * 8 + i
            staged[:, pl.ds(f * 256, 256)] = dot(att[...], obuf[f % 2, f // 2]).astype(BF16)
        out_copy(part).start()

    @pl.loop(1, NF)
    def _(k):
        a2a(lax.rem(me + k, NF)).wait_send()

    @pl.loop(1, 16)
    def _(k):
        ow_to(k).wait_send()

    for stage in range(2):
        for phase in range(5):
            for kind in range(4):
                for half in range(2):
                    ring(stage, half, phase, kind, True).wait_send()
        for dx in range(4):
            for dy in range(4):
                side(stage, dx, dy, c).wait_send()
    for step in range(1, 5):
        if step < 4:
            oz(0, step, True).wait_send()
        oz(1, step, True).wait_send()
        kv(step, True).wait_send()
    for back in range(NZ):
        o_side(back, c).wait_send()
    nm_out.wait()
    for part in range(4):
        out_copy(part).wait()


def rotation_tables():
    inverse = theta_base ** (-2.0 * np.arange(HD // 2, dtype=np.float64) / HD)
    inverse = np.concatenate([inverse, inverse])[None, :]
    low = np.arange(ROWS, dtype=np.float64)[:, None] * inverse
    high = np.arange(NZ, dtype=np.float64)[:, None] * ROWS * inverse
    return [t.astype(np.float32) for t in (np.cos(low), np.sin(low), np.cos(high), np.sin(high))]


def per_device(tokens, norm_gain, old_master, route_peer, route_slot, out_weight, doc_lengths):
    pad = ((0, 0), (0, LANES - route_peer.shape[1]))
    vmem = pl.BlockSpec(memory_space=pltpu.VMEM)
    hbm = pl.BlockSpec(memory_space=pl.ANY)
    dma = pltpu.SemaphoreType.DMA
    update, new_master = pl.pallas_call(
        kernel,
        out_shape=(jax.ShapeDtypeStruct((ROWS, D), BF16), jax.ShapeDtypeStruct((96, BLK), F32)),
        in_specs=[hbm, vmem, vmem, vmem, vmem, hbm, pl.BlockSpec(memory_space=pltpu.SMEM)] + [vmem] * 4,
        out_specs=(hbm, hbm),
        scratch_shapes=[
            pltpu.VMEM((ROWS, D), BF16),
            pltpu.VMEM((8 * LANES, 256), BF16),
            pltpu.VMEM((NF * 16, W), BF16),
            pltpu.VMEM((NF * 16, W), BF16),
            pltpu.VMEM((D, W), BF16),
            pltpu.VMEM((2, 16, 512, 256), BF16),
            pltpu.VMEM(((BACK + 1) * ROWS, 256), BF16),
            pltpu.VMEM((ROWS, W), F32),
            pltpu.VMEM((ROWS, QW), BF16),
            pltpu.VMEM((ROWS, D), BF16),
            pltpu.VMEM((96, BLK), F32),
            pltpu.VMEM((ROWS, (BACK + 1) * ROWS), F32),
            dma((3,)),
            dma((NF,)), dma((NF,)),
            dma((80,)), dma((80,)),
            dma((32,)), dma((32,)),
            dma((16,)), dma((16,)),
            dma((8,)), dma((8,)),
            dma((8,)), dma((8,)),
            dma((4,)), dma((4,)),
            dma((4,)),
        ],
        compiler_params=pltpu.CompilerParams(
            collective_id=0, has_side_effects=True, vmem_limit_bytes=56 * 1024 * 1024
        ),
        cost_estimate=pl.CostEstimate(flops=8 * 10**9, bytes_accessed=10**7, transcendentals=1310720),
    )(
        tokens[0],
        norm_gain[None, :],
        old_master,
        jnp.pad(route_peer, pad, constant_values=-1),
        jnp.pad(route_slot, pad, constant_values=-1),
        out_weight,
        doc_lengths,
        *rotation_tables(),
    )
    return (update[None], new_master)


def solution(mesh):
    placed = (
        P("fsdp", "dp", None),
        P(),
        P("fsdp", None),
        P(),
        P(),
        P(None, "fsdp"),
        P("fsdp", None),
    )
    return jax.shard_map(
        per_device,
        mesh=mesh,
        in_specs=placed,
        out_specs=(P("fsdp", "dp", None), P("fsdp", None)),
        check_vma=False,
    )
```

time: 204 us -> 111 us (0.54)
  the two profiles are of different devices: /device:TPU:2 before, /device:TPU:3 now
where the time goes in v1:
time: 111 us; the launch traced here: 110 us
  Pallas kernels  101 us (91%)
  local copies, waits for them, and re-layouts  8.25 us (7%)
    pallas_call x1, Pallas kernels, per_device(): pl.pallas_call(kernel, out_shape=(jax.ShapeDtypeStruct((ROWS, D), BF16),...  101 us
    unnamed x4, local copies, waits for them, and re-layouts  5.6 us

profile of v1, /device:TPU:3, one launch (start us, length us, event | category | flops | bytes accessed | tf_op | source)
XLA Modules:
  0.0 110.3 jit_solution(2350509217538904138)
XLA Ops:
  0.6 1.3 %pad.7.peer = s32[32,128]{1,0:T(8,128)} pad(s32[32,96]{1,0:T(8,128)} %param.14, s32[]{:T(128)} %constant.4.clone.1), padding=0_0x0_32 | pad | bytes 28676 | tf_op jit(solution)/shard_map/jit(_pad)/pad | solution.py:491
  2.0 1.3 %pad.8.slot = s32[32,128]{1,0:T(8,128)} pad(s32[32,96]{1,0:T(8,128)} %param.15, s32[]{:T(128)} %constant.4.clone.1), padding=0_0x0_32 | pad | bytes 28676 | tf_op jit(solution)/shard_map/jit(_pad)/pad | solution.py:492
  3.3 101.4 %shard_map.122 = (bf16[256,8192]{1,0:T(8,128)(2,1)}, f32[96,2048]{1,0:T(8,128)}) custom-call(bf16[256,8192]{1,0:T(8,128)(2,1)} %bitcast.4, f32[1,8192]{1,0:T(1,128)} %bitcast.5, f32[96,2048]{1,0:T(8,128)} %old.1, s32[32,128]{1,0:T(8,128)} %pad.7.peer, s32[32,128]{1,0:T(8,128)} %pad.8.slot, bf16[512,256]{1,0:T(8,128)(2,1)} %ow_hbm.1, s32[1,8]{1,0:T(1,128)} %docs.1, ...), custom_call_target="tpu_custom_call" | custom-call | flops 8000000000 | bytes 10000000 | tf_op jit(solution)/shard_map/pallas_call | solution.py:455
  104.7 0.0 copy-start
  104.8 4.7 %copy.15 = bf16[1,256,8192]{2,1,0:T(8,128)(2,1)} copy(bf16[1,256,8192]{2,1,0:T(8,128)(2,1)} %bitcast.3) | data formatting | bytes 8388608
  109.5 0.0 copy-done
  109.5 0.9 copy.16
Async XLA Ops:
  104.7 4.7 %copy-start = (f32[96,2048]{1,0:T(8,128)S(1)}, f32[96,2048]{1,0:T(8,128)}, u32[]{:S(2)}) copy-start(f32[96,2048]{1,0:T(8,128)} %get-tuple-element.9) | copy-start | bytes 2359300

commit v2 on v1

--- a/solution.py
+++ b/solution.py
@@ -20,6 +20,9 @@
 QW, KVW, W = 512, 256, 768
 LANES = 128
 COLS = ((QW, KVW), (0, QW))
+OZ = 64
+UP, DOWN = 3, 4
+PARTS = 4
 BACK = 4
 
 
@@ -36,10 +39,10 @@
 
 
 def kernel(
-    tok_hbm, gain, old, peer, slot, ow_hbm, docs, cos_r, sin_r, cos_z, sin_z,
-    out_hbm, nm_hbm,
-    tok, oldb, sendbuf, inbuf, wbuf, obuf, kvbuf, acc, att, staged, nm, bias,
-    local_sem, a2a_s, a2a_r, w_s, w_r, sib_s, sib_r, ow_s, ow_r, oz_s, oz_r, os_s, os_r, kv_s, kv_r, out_sem,
+    tok_hbm, gain, old, peer_in, slot_in, ow_hbm, docs, cos_r, sin_r, cos_z, sin_z,
+    att, obuf, nm,
+    tok, peer, slot, oldb, spread, blocks, sendbuf, inbuf, wbuf, kvbuf, acc, bias,
+    local_sem, a2a_s, a2a_r, w_s, w_r, sib_s, sib_r, ow_s, ow_r, oz_s, oz_r, os_s, os_r, kv_s, kv_r,
 ):
     me = lax.axis_index("fsdp")
     z = lax.axis_index("dp")
@@ -58,6 +61,8 @@
             src_ref=src, dst_ref=dst, send_sem=send, recv_sem=recv, device_id=to, device_id_type=MESH
         )
 
+    kvbuf[pl.ds(ROWS, BACK * ROWS), :] = jnp.zeros((BACK * ROWS, 256), BF16)
+
     barrier = pltpu.get_barrier_semaphore()
 
     @pl.loop(1, NF)
@@ -69,9 +74,12 @@
 
     tokens_in = pltpu.make_async_copy(tok_hbm, tok, local_sem.at[0])
     tokens_in.start()
-    own_rows = pl.ds(pl.multiple_of(z * 64, 64), 64)
+    own_rows = pl.ds(pl.multiple_of(z * OZ, 16), OZ)
     own_out = pltpu.make_async_copy(ow_hbm.at[own_rows, :], obuf.at[c, place, own_rows, :], local_sem.at[1])
     own_out.start()
+    for padded, given in ((peer, peer_in), (slot, slot_in)):
+        padded[...] = jnp.full_like(padded, -1)
+        padded[:, pl.ds(0, 96)] = given[...]
 
     for part in range(8):
         oldb[pl.ds(part * LANES, 96), :] = old[:, pl.ds(part * 256, 256)].astype(BF16)
@@ -80,33 +88,7 @@
     own_peer = peer[pl.ds(me, 1), :]
     mine = iota((NF, LANES), 0) == own_peer
     rank = jnp.sum(jnp.where(mine, dot(hot(mine), before), 0.0), axis=0, keepdims=True).astype(I32)
-    base = jnp.where(own_peer >= 0, own_peer * 16 + (rank & 1) * 8, -1000)
-    for g in range(3):
-        target = jnp.where((rank >> 1) == g, base, -1000)
-        rows = iota((NF * 16, LANES), 0)
-        select = jnp.concatenate([hot(rows == target + part) for part in range(8)], axis=1)
-        sendbuf[:, pl.ds(g * 256, 256)] = dot(select, oldb[...]).astype(BF16)
-
     pl.semaphore_wait(barrier, NF - 1 + 2)
-
-    def sixteen(f):
-        return pl.ds(pl.multiple_of(f * 16, 16), 16)
-
-    def a2a(to):
-        return remote(
-            sendbuf.at[sixteen(to), :], inbuf.at[sixteen(me), :], a2a_s.at[to], a2a_r.at[me], fsdp=to
-        )
-
-    def a2a_from(f):
-        return remote(
-            sendbuf.at[sixteen(f), :], inbuf.at[sixteen(f), :], a2a_s.at[f], a2a_r.at[f], fsdp=f
-        )
-
-    @pl.loop(1, NF)
-    def _(k):
-        a2a(lax.rem(me + k, NF)).start()
-
-    inbuf[sixteen(me), :] = sendbuf[sixteen(me), :]
 
     def ow_to(k):
         to = lax.rem(place + k, 16)
@@ -122,6 +104,80 @@
     @pl.loop(1, 16)
     def _(k):
         ow_to(k).start()
+
+    for g in range(3):
+        target = jnp.where((own_peer >= 0) & ((rank >> 1) == g), own_peer * 2 + (rank & 1), -1)
+        select = hot(iota((NF * 2, LANES), 0) == target)
+        for part in range(8):
+            block = dot(select, oldb[pl.ds(part * LANES, LANES), :])
+            for h in range(2):
+                spread[g * 2 + h, pl.ds(part, NF * 2, stride=8), :] = block[:, h * LANES : (h + 1) * LANES]
+    for t in range(6):
+        sendbuf[:, pl.ds(t * LANES, LANES)] = spread[t].astype(BF16)
+
+    def sixteen(f):
+        return pl.ds(pl.multiple_of(f * 16, 16), 16)
+
+    def a2a(to):
+        return remote(
+            sendbuf.at[sixteen(to), :], inbuf.at[sixteen(me), :], a2a_s.at[to], a2a_r.at[me], fsdp=to
+        )
+
+    def a2a_from(f):
+        return remote(
+            sendbuf.at[sixteen(f), :], inbuf.at[sixteen(f), :], a2a_s.at[f], a2a_r.at[f], fsdp=f
+        )
+
+    order = [(dx, dy, dc) for dx in range(4) for dy in range(4) for dc in range(2)][1:]
+    for dx, dy, dc in sorted(order, key=lambda t: -(t[0] & 1) - (t[1] & 1) - 2 * (t[0] == 2) - 2 * (t[1] == 2)):
+        a2a(panel(dx, dy, 1 - c if dc else c)).start()
+
+    inbuf[sixteen(me), :] = sendbuf[sixteen(me), :]
+
+    def oz_ref(at, core, part):
+        rows = pl.ds(pl.multiple_of(lax.rem(at + NZ, NZ) * OZ, 16), OZ)
+        return obuf.at[core, pl.ds(part * (16 // PARTS), 16 // PARTS), rows, :]
+
+    def oz(way, step, part, sending):
+        hops = step - 1 if sending else step
+        ref = oz_ref(z - hops if way == 0 else z + hops, c, part)
+        index = (way * UP + step - 1) * PARTS + part
+        return remote(ref, ref, oz_s.at[index], oz_r.at[index], dp=up if way == 0 else down)
+
+    def o_side(back, part, core):
+        ref = oz_ref(z - back, core, part)
+        index = back * PARTS + part
+        return remote(ref, ref, os_s.at[index], os_r.at[index], fsdp=sibling)
+
+    def oz_next(step, part):
+        if step <= UP:
+            oz(0, step, part, False).wait_recv()
+            if step < UP:
+                oz(0, step + 1, part, True).start()
+            o_side(step, part, c).start()
+        oz(1, step, part, False).wait_recv()
+        if step < DOWN:
+            oz(1, step + 1, part, True).start()
+        o_side(NZ - step, part, c).start()
+
+    events = iter([(step, part) for step in range(1, DOWN + 1) for part in range(PARTS)])
+
+    def oz_events(count):
+        for _ in range(count):
+            event = next(events, None)
+            if event:
+                oz_next(*event)
+
+    @pl.loop(1, 16)
+    def _(k):
+        ow_from(lax.rem(place + 16 - k, 16)).wait_recv()
+
+    own_out.wait()
+    for part in range(PARTS):
+        oz(0, 1, part, True).start()
+        oz(1, 1, part, True).start()
+    for part in range(PARTS):
+        o_side(0, part, c).start()
 
     tokens_in.wait()
 
@@ -134,17 +190,16 @@
 
     ours = peer[...] == me
     arrival = dot(hot(ours), before)
-    lane = iota((1, NF * 16), 1)
-    holder = iota((NF, NF * 16), 0) == (iota((NF, NF * 16), 1) >> 4)
-    odd = ((iota((NF, NF * 16), 1) >> 3) & 1) == 1
+    holder = iota((NF, NF * 2), 0) == (iota((NF, NF * 2), 1) >> 1)
+    odd = (iota((NF, NF * 2), 1) & 1) == 1
     slots = []
     for r in range(6):
         found = ours & (arrival == float(r))
         slots.append(jnp.sum(jnp.where(found, slot[...] + 1, 0), axis=1, keepdims=True) - 1)
-    slot_rows = []
+    selects = []
     for g in range(3):
-        spread = jnp.where(odd, slots[2 * g + 1], slots[2 * g])
-        slot_rows.append(jnp.sum(jnp.where(holder, spread, 0), axis=0, keepdims=True))
+        places = jnp.sum(jnp.where(holder, jnp.where(odd, slots[2 * g + 1], slots[2 * g]), 0), axis=0, keepdims=True)
+        selects.append(hot(iota((96, NF * 2), 0) == places))
 
     @pl.loop(1, NF)
     def _(k):
@@ -153,14 +208,24 @@
     def panel_rows(f):
         return pl.ds(pl.multiple_of(f * ROWS, ROWS), ROWS)
 
-    for g in range(3):
-        total = jnp.zeros((256, 256), F32)
-        for h in range(3):
-            flat = slot_rows[h] * 8 + (lane & 7)
-            row = (flat * 21846) >> 16
-            row = jnp.where((slot_rows[h] >= 0) & (flat - row * 3 == g), row, -1)
-            total += dot(hot(iota((256, NF * 16), 0) == row), inbuf[:, pl.ds(h * 256, 256)])
-        wbuf[panel_rows(me), pl.ds(g * 256, 256)] = total.astype(BF16)
+    for t in range(6):
+        spread[t] = inbuf[:, pl.ds(t * LANES, LANES)].astype(F32)
+    for part in range(8):
+        for h in range(2):
+            total = jnp.zeros((96, LANES), F32)
+            for g in range(3):
+                piece = spread[g * 2 + h, pl.ds(part, NF * 2, stride=8), :].astype(BF16)
+                total += dot(selects[g], piece)
+            nm[:, pl.ds((part * 2 + h) * LANES, LANES)] = total
+            blocks[part * 2 + h] = total
+    for k in range(3):
+        for part in range(8):
+            row, third = divmod(8 * k + part, 3)
+            for h in range(2):
+                piece = blocks[part * 2 + h, pl.ds(k, 32, stride=3), :]
+                spread[third * 2 + h, pl.ds(row, 32, stride=8), :] = piece
+    for t in range(6):
+        wbuf[panel_rows(me), pl.ds(t * LANES, LANES)] = spread[t, pl.ds(0, ROWS), :].astype(BF16)
 
     def coords(half, first, second):
         return (first, second) if half == 0 else (second, first)
@@ -273,75 +338,58 @@
         come(stage, 3, (2, 3))
         share(stage, far)
 
-    def oz(way, step, sending):
-        at = z - (step - 1 if sending else step) if way == 0 else z + (step - 1 if sending else step)
-        rows = pl.ds(pl.multiple_of(lax.rem(at + NZ, NZ) * 64, 64), 64)
-        ref = obuf.at[c, :, rows, :]
-        index = way * 4 + step - 1
-        return remote(ref, ref, oz_s.at[index], oz_r.at[index], dp=up if way == 0 else down)
-
-    def o_side(back, core):
-        rows = pl.ds(pl.multiple_of(lax.rem(z + NZ - back, NZ) * 64, 64), 64)
-        ref = obuf.at[core, :, rows, :]
-        return remote(ref, ref, os_s.at[back], os_r.at[back], fsdp=sibling)
-
-    def oz_next(step):
-        if step <= 3:
-            oz(0, step, False).wait_recv()
-            if step < 3:
-                oz(0, step + 1, True).start()
-            o_side(step, c).start()
-        oz(1, step, False).wait_recv()
-        if step < 4:
-            oz(1, step + 1, True).start()
-        o_side(NZ - step, c).start()
-
-    def kv(step, sending):
+    def kv(step):
         src = kvbuf.at[pl.ds((step - 1) * ROWS, ROWS), :]
         dst = kvbuf.at[pl.ds(step * ROWS, ROWS), :]
         return remote(src, dst, kv_s.at[step - 1], kv_r.at[step - 1], dp=up)
 
+    def kv_send(step):
+        @pl.when((z < NZ - 1) & (z >= step - 1))
+        def _():
+            kv(step).start()
+
+    def kv_sent(step):
+        @pl.when((z < NZ - 1) & (z >= step - 1))
+        def _():
+            kv(step).wait_send()
+
+    def kv_next(step):
+        @pl.when(z >= step)
+        def _():
+            kv(step).wait_recv()
+
+        if step < BACK:
+            kv_send(step + 1)
+
     open_stage(0)
-
-    @pl.loop(1, 16)
-    def _(k):
-        ow_from(lax.rem(place + 16 - k, 16)).wait_recv()
-
-    own_out.wait()
-    oz(0, 1, True).start()
-    oz(1, 1, True).start()
-    o_side(0, c).start()
-
+    acc[...] = jnp.zeros_like(acc)
+    oz_events(3)
     step_one(0)
-    acc[...] = jnp.zeros_like(acc)
-    for part in range(8):
-        total = jnp.zeros((96, 256), F32)
-        for h in range(3):
-            row = jnp.where((lane & 7) == part, slot_rows[h], -1)
-            total += dot(hot(iota((96, NF * 16), 0) == row), inbuf[:, pl.ds(h * 256, 256)])
-        nm[:, pl.ds(part * 256, 256)] = total
-    nm_out = pltpu.make_async_copy(nm, nm_hbm, local_sem.at[2])
-    nm_out.start()
     step_two(0)
+    oz_events(2)
     multiply(0, near, False)
+    open_stage(1)
     step_three(0)
     multiply(0, near, True)
-    open_stage(1)
     step_four(0)
     multiply(0, cross, False)
+    oz_events(2)
     step_five(0)
     multiply(0, cross, True)
     multiply(0, corner, False)
+    oz_events(1)
     step_one(1)
     step_six(0)
-    oz_next(1)
     multiply(0, corner + two, True)
-    multiply(0, two, False)
+    multiply(0, two + knight, False)
+    oz_events(1)
     step_two(1)
     step_seven(0)
-    multiply(0, knight + far, False)
+    multiply(0, far, False)
+    multiply(0, knight, True)
+    oz_events(1)
     step_three(1)
-    multiply(0, knight + far, True)
+    multiply(0, far, True)
 
     cz, sz = cos_z[pl.ds(z, 1), :], sin_z[pl.ds(z, 1), :]
     cosine = cos_r[...] * cz - sin_r[...] * sz
@@ -353,21 +401,22 @@
 
     kvbuf[pl.ds(0, ROWS), pl.ds(0, HD)] = rotate(acc[:, pl.ds(QW, HD)])
     kvbuf[pl.ds(0, ROWS), pl.ds(HD, HD)] = acc[:, pl.ds(QW + HD, HD)].astype(BF16)
-    kv(1, True).start()
+    kv_send(1)
+    oz_events(1)
     step_four(1)
+    oz_events(1)
     multiply(1, near + cross, False)
-    kv(1, False).wait_recv()
-    kv(2, True).start()
+    kv_next(1)
     step_five(1)
-    oz_next(2)
+    oz_events(1)
     multiply(1, near + cross, True)
-    kv(2, False).wait_recv()
-    kv(3, True).start()
+    kv_next(2)
+    oz_events(1)
     multiply(1, corner + two, False)
     step_six(1)
+    oz_events(1)
     multiply(1, corner + two, True)
-    kv(3, False).wait_recv()
-    kv(4, True).start()
+    kv_next(3)
 
     query = z * ROWS + iota((ROWS, 1), 0)
     begin = jnp.zeros((ROWS, 1), I32)
@@ -379,13 +428,15 @@
         key = (z - back) * ROWS + iota((ROWS, ROWS), 1)
         bias[:, pl.ds(back * ROWS, ROWS)] = jnp.where((key <= query) & (key >= begin), 0.0, masked_score)
 
+    multiply(1, knight, False)
     step_seven(1)
-    oz_next(3)
-    multiply(1, knight + far, False)
-    multiply(1, knight + far, True)
-    kv(4, False).wait_recv()
-
-    scale = 1.0 / np.sqrt(np.float32(HD))
+    multiply(1, knight, True)
+    multiply(1, far, False)
+    oz_events(1)
+    multiply(1, far, True)
+    kv_next(4)
+
+    scale = np.float32(np.log2(np.e) / np.sqrt(HD))
     for h in range(HQ):
         columns = pl.ds(h * HD, HD)
         queries = rotate(acc[:, columns])
@@ -393,23 +444,16 @@
             queries, kvbuf[:, pl.ds(0, HD)], (((1,), (1,)), ((), ())), preferred_element_type=F32
         )
         scores = scores * scale + bias[...]
-        expterm = jnp.exp(scores - jnp.max(scores, axis=1, keepdims=True))
+        expterm = jnp.exp2(scores - jnp.max(scores, axis=1, keepdims=True))
         denom = jnp.sum(expterm, axis=1, keepdims=True)
         att[:, columns] = (dot(expterm.astype(BF16), kvbuf[:, pl.ds(HD, HD)]) / denom).astype(BF16)
-
-    oz_next(4)
-    for back in range(NZ):
-        o_side(back, 1 - c).wait_recv()
-
-    def out_copy(part):
-        columns = pl.ds(part * 2048, 2048)
-        return pltpu.make_async_copy(staged.at[:, columns], out_hbm.at[:, columns], out_sem.at[part])
-
-    for part in range(4):
-        for i in range(8):
-            f = part * 8 + i
-            staged[:, pl.ds(f * 256, 256)] = dot(att[...], obuf[f % 2, f // 2]).astype(BF16)
-        out_copy(part).start()
+        oz_events(1)
+
+    for event in events:
+        oz_next(*event)
+    for part in range(PARTS):
+        for back in range(NZ):
+            o_side(back, part, 1 - c).wait_recv()
 
     @pl.loop(1, NF)
     def _(k):
@@ -427,16 +471,29 @@
         for dx in range(4):
             for dy in range(4):
                 side(stage, dx, dy, c).wait_send()
-    for step in range(1, 5):
-        if step < 4:
-            oz(0, step, True).wait_send()
-        oz(1, step, True).wait_send()
-        kv(step, True).wait_send()
-    for back in range(NZ):
-        o_side(back, c).wait_send()
-    nm_out.wait()
-    for part in range(4):
-        out_copy(part).wait()
+    for part in range(PARTS):
+        for step in range(1, UP + 1):
+            oz(0, step, part, True).wait_send()
+        for step in range(1, DOWN + 1):
+            oz(1, step, part, True).wait_send()
+        for back in range(NZ):
+            o_side(back, part, c).wait_send()
+    for step in range(1, BACK + 1):
+        kv_sent(step)
+
+
+def project(att, weight, nm_in, out, nm, staged, sem):
+    routed = pltpu.make_async_copy(nm_in, nm, sem.at[8])
+    routed.start()
+    copies = [routed]
+    for part in range(8):
+        for f in range(part * 4, part * 4 + 4):
+            staged[:, pl.ds(f * 256, 256)] = dot(att[...], weight[f % 2, f // 2]).astype(BF16)
+        columns = pl.ds(part * 1024, 1024)
+        copies.append(pltpu.make_async_copy(staged.at[:, columns], out.at[:, columns], sem.at[part]))
+        copies[-1].start()
+    for copy in copies:
+        copy.wait()
 
 
 def rotation_tables():
@@ -448,52 +505,63 @@
 
 
 def per_device(tokens, norm_gain, old_master, route_peer, route_slot, out_weight, doc_lengths):
-    pad = ((0, 0), (0, LANES - route_peer.shape[1]))
     vmem = pl.BlockSpec(memory_space=pltpu.VMEM)
     hbm = pl.BlockSpec(memory_space=pl.ANY)
     dma = pltpu.SemaphoreType.DMA
-    update, new_master = pl.pallas_call(
+    attended, gathered, routed = pl.pallas_call(
         kernel,
-        out_shape=(jax.ShapeDtypeStruct((ROWS, D), BF16), jax.ShapeDtypeStruct((96, BLK), F32)),
+        out_shape=(
+            pltpu.VMEM((ROWS, QW), BF16),
+            pltpu.VMEM((2, 16, 512, 256), BF16),
+            pltpu.VMEM((96, BLK), F32),
+        ),
         in_specs=[hbm, vmem, vmem, vmem, vmem, hbm, pl.BlockSpec(memory_space=pltpu.SMEM)] + [vmem] * 4,
-        out_specs=(hbm, hbm),
+        out_specs=(vmem, vmem, vmem),
         scratch_shapes=[
             pltpu.VMEM((ROWS, D), BF16),
+            pltpu.VMEM((NF, LANES), I32),
+            pltpu.VMEM((NF, LANES), I32),
             pltpu.VMEM((8 * LANES, 256), BF16),
+            pltpu.VMEM((6, NF * 16, LANES), F32),
+            pltpu.VMEM((16, 96, LANES), F32),
             pltpu.VMEM((NF * 16, W), BF16),
             pltpu.VMEM((NF * 16, W), BF16),
             pltpu.VMEM((D, W), BF16),
-            pltpu.VMEM((2, 16, 512, 256), BF16),
             pltpu.VMEM(((BACK + 1) * ROWS, 256), BF16),
             pltpu.VMEM((ROWS, W), F32),
-            pltpu.VMEM((ROWS, QW), BF16),
-            pltpu.VMEM((ROWS, D), BF16),
-            pltpu.VMEM((96, BLK), F32),
             pltpu.VMEM((ROWS, (BACK + 1) * ROWS), F32),
             dma((3,)),
             dma((NF,)), dma((NF,)),
             dma((80,)), dma((80,)),
             dma((32,)), dma((32,)),
             dma((16,)), dma((16,)),
-            dma((8,)), dma((8,)),
-            dma((8,)), dma((8,)),
+            dma(((UP + DOWN) * PARTS,)), dma(((UP + DOWN) * PARTS,)),
+            dma((NZ * PARTS,)), dma((NZ * PARTS,)),
             dma((4,)), dma((4,)),
-            dma((4,)),
         ],
         compiler_params=pltpu.CompilerParams(
-            collective_id=0, has_side_effects=True, vmem_limit_bytes=56 * 1024 * 1024
+            collective_id=0, has_side_effects=True, vmem_limit_bytes=50 * 1024 * 1024
         ),
         cost_estimate=pl.CostEstimate(flops=8 * 10**9, bytes_accessed=10**7, transcendentals=1310720),
     )(
         tokens[0],
         norm_gain[None, :],
         old_master,
-        jnp.pad(route_peer, pad, constant_values=-1),
-        jnp.pad(route_slot, pad, constant_values=-1),
+        route_peer,
+        route_slot,
         out_weight,
         doc_lengths,
         *rotation_tables(),
     )
+    update, new_master = pl.pallas_call(
+        project,
+        out_shape=(jax.ShapeDtypeStruct((ROWS, D), BF16), jax.ShapeDtypeStruct((96, BLK), F32)),
+        in_specs=[vmem, vmem, vmem],
+        out_specs=(hbm, hbm),
+        scratch_shapes=[pltpu.VMEM((ROWS, D), BF16), dma((9,))],
+        compiler_params=pltpu.CompilerParams(vmem_limit_bytes=16 * 1024 * 1024),
+        cost_estimate=pl.CostEstimate(flops=2 * ROWS * QW * D, bytes_accessed=5 * 10**6, transcendentals=0),
+    )(attended, gathered, routed)
     return (update[None], new_master)
 
 

time: 111 us -> 84.9 us (0.76)
  the two profiles are of different devices: /device:TPU:3 before, /device:TPU:224 now
where the time goes in v2:
time: 84.9 us; the launch traced here: 84.7 us
  Pallas kernels  83.9 us (99%)
    pallas_call x1, Pallas kernels, per_device(): pl.pallas_call(kernel, out_shape=(pltpu.VMEM((ROWS, QW), BF16), pltpu.VME...  80.7 us
    pallas_call x1, Pallas kernels, per_device(): pl.pallas_call(project, out_shape=(jax.ShapeDtypeStruct((ROWS, D), BF16),...  3.22 us

profile of v2, /device:TPU:224, one launch (start us, length us, event | category | flops | bytes accessed | tf_op | source)
XLA Modules:
  0.0 84.7 jit_solution(919470236125348737)
XLA Ops:
  0.6 80.7 %shard_map.122 = (bf16[256,512]{1,0:T(8,128)(2,1)S(1)}, bf16[2,16,512,256]{3,2,1,0:T(8,128)(2,1)S(1)}, f32[96,2048]{1,0:T(8,128)S(1)}) custom-call(bf16[256,8192]{1,0:T(8,128)(2,1)} %bitcast.3, f32[1,8192]{1,0:T(1,128)} %bitcast.5, f32[96,2048]{1,0:T(8,128)} %old.1, s32[32,96]{1,0:T(8,128)} %peer_in.1, s32[32,96]{1,0:T(8,128)} %slot_in.1, ...), custom_call_target="tpu_custom_call" | custom-call | flops 8000000000 | bytes 10000000 | tf_op jit(solution)/shard_map/pallas_call | solution.py:511
  81.4 3.2 %shard_map.123 = (bf16[256,8192]{1,0:T(8,128)(2,1)}, f32[96,2048]{1,0:T(8,128)}) custom-call(bf16[256,512]{1,0:T(8,128)(2,1)S(1)} %get-tuple-element.7.att, bf16[2,16,512,256]{3,2,1,0:T(8,128)(2,1)S(1)} %get-tuple-element.8.weight, f32[96,2048]{1,0:T(8,128)S(1)} %get-tuple-element.9.nm_in), custom_call_target="tpu_custom_call" | custom-call | flops 2147483648 | bytes 5000000 | tf_op jit(solution)/shard_map/pallas_call | solution.py:556

commit v3 on v2

--- a/solution.py
+++ b/solution.py
@@ -187,6 +187,16 @@
         values = tok[rows, :].astype(F32)
         square_mean = jnp.mean(values * values, axis=-1, keepdims=True)
         tok[rows, :] = (values * lax.rsqrt(square_mean + epsilon) * gain[...]).astype(BF16)
+
+    query = z * ROWS + iota((ROWS, 1), 0)
+    begin = jnp.zeros((ROWS, 1), I32)
+    end = jnp.int32(0)
+    for d in range(8):
+        end = end + docs[0, d]
+        begin = jnp.where(query >= end, end, begin)
+    for back in range(BACK + 1):
+        key = (z - back) * ROWS + iota((ROWS, ROWS), 1)
+        bias[:, pl.ds(back * ROWS, ROWS)] = jnp.where((key <= query) & (key >= begin), 0.0, masked_score)
 
     ours = peer[...] == me
     arrival = dot(hot(ours), before)
@@ -275,12 +285,14 @@
 
     def multiply(stage, places, other):
         first, width = COLS[stage]
-        for dx, dy in places:
-            if other:
+        columns = pl.ds(first, width)
+        if other:
+            for dx, dy in places:
                 side(stage, dx, dy, 1 - c).wait_recv()
-            f = panel(dx, dy, 1 - c if other else c)
-            columns = pl.ds(first, width)
-            acc[:, columns] += dot(tok[:, panel_rows(f)], wbuf[panel_rows(f), columns])
+        rows = [panel_rows(panel(dx, dy, 1 - c if other else c)) for dx, dy in places]
+        left = jnp.concatenate([tok[:, r] for r in rows], axis=1)
+        right = jnp.concatenate([wbuf[r, columns] for r in rows], axis=0)
+        acc[:, columns] += dot(left, right)
 
     near = [(0, 0)]
     cross = [(1, 0), (3, 0), (0, 1), (0, 3)]
@@ -363,17 +375,19 @@
 
     open_stage(0)
     acc[...] = jnp.zeros_like(acc)
-    oz_events(3)
+    oz_events(2)
     step_one(0)
+    oz_events(1)
     step_two(0)
-    oz_events(2)
+    oz_events(1)
     multiply(0, near, False)
     open_stage(1)
     step_three(0)
     multiply(0, near, True)
     step_four(0)
+    oz_events(1)
     multiply(0, cross, False)
-    oz_events(2)
+    oz_events(1)
     step_five(0)
     multiply(0, cross, True)
     multiply(0, corner, False)
@@ -385,8 +399,8 @@
     oz_events(1)
     step_two(1)
     step_seven(0)
+    multiply(0, knight, True)
     multiply(0, far, False)
-    multiply(0, knight, True)
     oz_events(1)
     step_three(1)
     multiply(0, far, True)
@@ -402,37 +416,28 @@
     kvbuf[pl.ds(0, ROWS), pl.ds(0, HD)] = rotate(acc[:, pl.ds(QW, HD)])
     kvbuf[pl.ds(0, ROWS), pl.ds(HD, HD)] = acc[:, pl.ds(QW + HD, HD)].astype(BF16)
     kv_send(1)
+    multiply(1, near + cross, False)
     oz_events(1)
     step_four(1)
-    oz_events(1)
-    multiply(1, near + cross, False)
+    multiply(1, near + cross, True)
+    oz_events(1)
+    multiply(1, corner, False)
     kv_next(1)
     step_five(1)
     oz_events(1)
-    multiply(1, near + cross, True)
+    multiply(1, corner, True)
+    multiply(1, two, False)
     kv_next(2)
     oz_events(1)
-    multiply(1, corner + two, False)
     step_six(1)
-    oz_events(1)
-    multiply(1, corner + two, True)
+    multiply(1, knight, False)
+    multiply(1, two, True)
+    oz_events(1)
     kv_next(3)
-
-    query = z * ROWS + iota((ROWS, 1), 0)
-    begin = jnp.zeros((ROWS, 1), I32)
-    end = jnp.int32(0)
-    for d in range(8):
-        end = end + docs[0, d]
-        begin = jnp.where(query >= end, end, begin)
-    for back in range(BACK + 1):
-        key = (z - back) * ROWS + iota((ROWS, ROWS), 1)
-        bias[:, pl.ds(back * ROWS, ROWS)] = jnp.where((key <= query) & (key >= begin), 0.0, masked_score)
-
-    multiply(1, knight, False)
     step_seven(1)
     multiply(1, knight, True)
+    oz_events(1)
     multiply(1, far, False)
-    oz_events(1)
     multiply(1, far, True)
     kv_next(4)
 

time: 84.9 us -> 82.5 us (0.972); the launches traced: 84.7 us -> 81.5 us
  Pallas kernels: 83.9 us -> 80.7 us
    pallas_call x1, Pallas kernels: 80.7 us -> 77.4 us  [per_device(): pl.pallas_call(kernel, out_shape=(pltpu.VMEM((ROWS, QW), BF16), pltpu.VME...]
where the time goes in v3:
time: 82.5 us; the launch traced here: 81.5 us
  Pallas kernels  80.7 us (98%)
    pallas_call x1, Pallas kernels, per_device(): pl.pallas_call(kernel, out_shape=(pltpu.VMEM((ROWS, QW), BF16), pltpu.VME...  77.4 us
    pallas_call x1, Pallas kernels, per_device(): pl.pallas_call(project, out_shape=(jax.ShapeDtypeStruct((ROWS, D), BF16),...  3.22 us

profile of v3, /device:TPU:224, one launch (start us, length us, event | category | flops | bytes accessed | tf_op | source)
XLA Modules:
  0.0 81.5 jit_solution(14454807251620026706)
XLA Ops:
  0.6 77.4 %shard_map.122 = (bf16[256,512]{1,0:T(8,128)(2,1)S(1)}, bf16[2,16,512,256]{3,2,1,0:T(8,128)(2,1)S(1)}, f32[96,2048]{1,0:T(8,128)S(1)}) custom-call(bf16[256,8192]{1,0:T(8,128)(2,1)} %bitcast.3, f32[1,8192]{1,0:T(1,128)} %bitcast.5, f32[96,2048]{1,0:T(8,128)} %old.1, s32[32,96]{1,0:T(8,128)} %peer_in.1, s32[32,96]{1,0:T(8,128)} %slot_in.1, ...), custom_call_target="tpu_custom_call" | custom-call | flops 8000000000 | bytes 10000000 | tf_op jit(solution)/shard_map/pallas_call | solution.py:516
  78.1 3.2 %shard_map.123 = (bf16[256,8192]{1,0:T(8,128)(2,1)}, f32[96,2048]{1,0:T(8,128)}) custom-call(bf16[256,512]{1,0:T(8,128)(2,1)S(1)} %get-tuple-element.7.att, bf16[2,16,512,256]{3,2,1,0:T(8,128)(2,1)S(1)} %get-tuple-element.8.weight, f32[96,2048]{1,0:T(8,128)S(1)} %get-tuple-element.9.nm_in), custom_call_target="tpu_custom_call" | custom-call | flops 2147483648 | bytes 5000000 | tf_op jit(solution)/shard_map/pallas_call | solution.py:561

commit v4 on v3

--- a/solution.py
+++ b/solution.py
@@ -402,7 +402,6 @@
     multiply(0, knight, True)
     multiply(0, far, False)
     oz_events(1)
-    step_three(1)
     multiply(0, far, True)
 
     cz, sz = cos_z[pl.ds(z, 1), :], sin_z[pl.ds(z, 1), :]
@@ -416,24 +415,25 @@
     kvbuf[pl.ds(0, ROWS), pl.ds(0, HD)] = rotate(acc[:, pl.ds(QW, HD)])
     kvbuf[pl.ds(0, ROWS), pl.ds(HD, HD)] = acc[:, pl.ds(QW + HD, HD)].astype(BF16)
     kv_send(1)
+    step_three(1)
     multiply(1, near + cross, False)
     oz_events(1)
     step_four(1)
+    kv_next(1)
     multiply(1, near + cross, True)
     oz_events(1)
     multiply(1, corner, False)
-    kv_next(1)
     step_five(1)
+    kv_next(2)
     oz_events(1)
     multiply(1, corner, True)
     multiply(1, two, False)
-    kv_next(2)
     oz_events(1)
     step_six(1)
+    kv_next(3)
     multiply(1, knight, False)
     multiply(1, two, True)
     oz_events(1)
-    kv_next(3)
     step_seven(1)
     multiply(1, knight, True)
     oz_events(1)

time: 82.5 us -> 80.6 us (0.977)
  Pallas kernels: 80.7 us -> 79.2 us
    pallas_call x1, Pallas kernels: 77.4 us -> 76 us  [per_device(): pl.pallas_call(kernel, out_shape=(pltpu.VMEM((ROWS, QW), BF16), pltpu.VME...]
where the time goes in v4:
time: 80.6 us; the launch traced here: 80 us
  Pallas kernels  79.2 us (98%)
    pallas_call x1, Pallas kernels, per_device(): pl.pallas_call(kernel, out_shape=(pltpu.VMEM((ROWS, QW), BF16), pltpu.VME...  76 us
    pallas_call x1, Pallas kernels, per_device(): pl.pallas_call(project, out_shape=(jax.ShapeDtypeStruct((ROWS, D), BF16),...  3.22 us

profile of v4, /device:TPU:224, one launch (start us, length us, event | category | flops | bytes accessed | tf_op | source)
XLA Modules:
  0.0 80.0 jit_solution(15604145839451213509)
XLA Ops:
  0.6 76.0 %shard_map.122 = (bf16[256,512]{1,0:T(8,128)(2,1)S(1)}, bf16[2,16,512,256]{3,2,1,0:T(8,128)(2,1)S(1)}, f32[96,2048]{1,0:T(8,128)S(1)}) custom-call(bf16[256,8192]{1,0:T(8,128)(2,1)} %bitcast.3, f32[1,8192]{1,0:T(1,128)} %bitcast.5, f32[96,2048]{1,0:T(8,128)} %old.1, s32[32,96]{1,0:T(8,128)} %peer_in.1, s32[32,96]{1,0:T(8,128)} %slot_in.1, ...), custom_call_target="tpu_custom_call" | custom-call | flops 8000000000 | bytes 10000000 | tf_op jit(solution)/shard_map/pallas_call | solution.py:516
  76.6 3.2 %shard_map.123 = (bf16[256,8192]{1,0:T(8,128)(2,1)}, f32[96,2048]{1,0:T(8,128)}) custom-call(bf16[256,512]{1,0:T(8,128)(2,1)S(1)} %get-tuple-element.7.att, bf16[2,16,512,256]{3,2,1,0:T(8,128)(2,1)S(1)} %get-tuple-element.8.weight, f32[96,2048]{1,0:T(8,128)S(1)} %get-tuple-element.9.nm_in), custom_call_target="tpu_custom_call" | custom-call | flops 2147483648 | bytes 5000000 | tf_op jit(solution)/shard_map/pallas_call | solution.py:561
